TPU v7x, 32 devices: a whole 2x2x4 slice. The times are simulated.
32 devices in a mesh: radial: 8 (over y, x, core), axial: 4 (over z).
Axes of the slice: x: 2, y: 2, z: 4, core: 2. Of those that a mesh axis runs over, the one named last changes fastest.
Arguments:
- rhs: float32 [2, 2, 96, 64, 512], P(None, None, None, 'radial', 'axial'), may hold values from -6 to 6
- mat_ids: int32 [96, 64, 512], P(None, 'radial', 'axial'), may hold values from 0 to 3
- stiff_table: float32 [4], replicated, may hold values from 0.5 to 4
- dens_table: float32 [4], replicated, may hold values from 0.5 to 2
- mass_shift: float32 [2], replicated, may hold values from 0.5 to 2
- harmonic: int32 [2], replicated, may hold values from 1 to 12
- radial_factor: float32 [2, 2, 16, 16], replicated, may hold values from -0.09375 to 0.09375
- axial_factor: float32 [2, 2, 64, 64], replicated, may hold values from -0.046875 to 0.046875
Outputs:
- solution: float32 [2, 2, 96, 64, 512], P(None, None, None, 'radial', 'axial')
- residual: float32 [2, 2, 96, 64, 512], P(None, None, None, 'radial', 'axial')
All inputs are finite; a program needn't handle non-finite values.
Results may differ from a plain program's by a relative error of at most 0.00021.
Values sent between devices are 32-bit elements; how exact they have to be, the bound alone decides.
A program may use at most 128 MiB of HBM per device.

v0:
```python
import jax
import jax.numpy as jnp
from jax import lax
from jax.sharding import PartitionSpec as P

ITERS = 3
NSECT = 24
AR = 4
AA = 8
LOSS_FACTOR = 0.2
RELAXATION = 0.6


def extended(shard, sides, width):
    for axis, dim in sides:
        size, length = (lax.axis_size(axis), shard.shape[dim])
        up = [(i, (i + 1) % size) for i in range(size - 1)]
        down = [(j, i) for i, j in up]
        last = lax.slice_in_dim(shard, length - width, length, axis=dim)
        first = lax.slice_in_dim(shard, 0, width, axis=dim)
        before = lax.ppermute(last, axis, up)
        after = lax.ppermute(first, axis, down)
        shard = jnp.concatenate([before, shard, after], axis=dim)
    return shard


def material(mat_ids, table):
    result = jnp.zeros(mat_ids.shape, table.dtype)
    for entry in range(table.shape[0]):
        result = result + jnp.where(mat_ids == entry, table[entry], jnp.zeros((), table.dtype))
    return result


def couplings(stiffness, padded):
    return (
        0.5 * (stiffness + padded[:, 2:, 1:-1]),
        0.5 * (stiffness + padded[:, :-2, 1:-1]),
        0.5 * (stiffness + padded[:, 1:-1, 2:]),
        0.5 * (stiffness + padded[:, 1:-1, :-2]),
        0.5 * (stiffness + jnp.roll(stiffness, -1, 0)),
        0.5 * (stiffness + jnp.roll(stiffness, 1, 0)),
    )


def neighbours(values, padded, weights, cosines, sines):
    summed = weights[0] * padded[:, :, :, 2:, 1:-1] + weights[1] * padded[:, :, :, :-2, 1:-1]
    summed = (
        summed + weights[2] * padded[:, :, :, 1:-1, 2:] + weights[3] * padded[:, :, :, 1:-1, :-2]
    )
    real_part = values[0]
    imag_part = values[1]
    cosine = cosines[:, None, None, None]
    sine = sines[:, None, None, None]
    wrap_real = cosine * real_part[:, :1] - sine * imag_part[:, :1]
    wrap_imag = sine * real_part[:, :1] + cosine * imag_part[:, :1]
    ahead = jnp.stack(
        [
            jnp.concatenate([real_part[:, 1:], wrap_real], 1),
            jnp.concatenate([imag_part[:, 1:], wrap_imag], 1),
        ]
    )
    back_real = cosine * real_part[:, -1:] + sine * imag_part[:, -1:]
    back_imag = cosine * imag_part[:, -1:] - sine * real_part[:, -1:]
    behind = jnp.stack(
        [
            jnp.concatenate([back_real, real_part[:, :-1]], 1),
            jnp.concatenate([back_imag, imag_part[:, :-1]], 1),
        ]
    )
    return summed + weights[4] * ahead + weights[5] * behind


def operate(values, weights, diag_real, diag_imag, cosines, sines):
    padded = extended(values, (("radial", 3), ("axial", 4)), 1)
    coupled = neighbours(values, padded, weights, cosines, sines)
    real_out = (
        diag_real * values[0] - diag_imag * values[1] - (coupled[0] - LOSS_FACTOR * coupled[1])
    )
    imag_out = (
        diag_real * values[1] + diag_imag * values[0] - (coupled[1] + LOSS_FACTOR * coupled[0])
    )
    return jnp.stack([real_out, imag_out])


def right_product(left_real, left_imag, right_real, right_imag):

    def matmul(first, second):
        return jnp.einsum("hij,hkj->hik", first, second, precision=lax.Precision.HIGHEST)

    return (
        matmul(left_real, right_real) - matmul(left_imag, right_imag),
        matmul(left_real, right_imag) + matmul(left_imag, right_real),
    )


def left_product(left_real, left_imag, right_real, right_imag):

    def matmul(first, second):
        return jnp.einsum("hij,hjk->hik", first, second, precision=lax.Precision.HIGHEST)

    return (
        matmul(left_real, right_real) - matmul(left_imag, right_imag),
        matmul(left_real, right_imag) + matmul(left_imag, right_real),
    )


def jacobi_step(residual, diag_real, diag_imag):
    scale = RELAXATION / (diag_real * diag_real + diag_imag * diag_imag)
    real_out = (diag_real * residual[0] + diag_imag * residual[1]) * scale
    imag_out = (diag_real * residual[1] - diag_imag * residual[0]) * scale
    return jnp.stack([real_out, imag_out])


def coarse_correction(residual, radial_factor, axial_factor):
    shape = residual.shape
    band_rows = shape[3] // AR
    band_cols = shape[4] // AA
    blocks = residual.reshape(2, shape[1], shape[2], band_rows, AR, band_cols, AA)
    coarse_res = jnp.sum(blocks, axis=(2, 4, 6))
    mine_axial = lax.dynamic_slice_in_dim(
        axial_factor, lax.axis_index("axial") * band_cols, band_cols, 2
    )
    mine_radial = lax.dynamic_slice_in_dim(
        radial_factor, lax.axis_index("radial") * band_rows, band_rows, 2
    )
    radial_count = lax.axis_size("radial")
    axial_count = lax.axis_size("axial")
    collected = lax.all_gather(coarse_res[None], ("radial", "axial"), axis=0, tiled=True)
    collected = collected.reshape(radial_count, axial_count, 2, shape[1], band_rows, band_cols)
    collected = collected.transpose(2, 3, 0, 4, 1, 5).reshape(
        2, shape[1], radial_count * band_rows, axial_count * band_cols
    )
    mixed_real, mixed_imag = right_product(collected[0], collected[1], mine_axial[0], mine_axial[1])
    corr_real, corr_imag = left_product(mine_radial[0], mine_radial[1], mixed_real, mixed_imag)
    spread = jnp.repeat(jnp.repeat(jnp.stack([corr_real, corr_imag]), AR, axis=2), AA, axis=3)
    return spread[:, :, None]


def local(rhs, mat_ids, stiff_table, dens_table, mass_shift, harmonic, radial_factor, axial_factor):
    stiffness = material(mat_ids, stiff_table)
    density = material(mat_ids, dens_table)
    padded_stiff = extended(stiffness, (("radial", 1), ("axial", 2)), 1)
    weights = couplings(stiffness, padded_stiff)
    total = weights[0] + weights[1] + weights[2] + weights[3] + weights[4] + weights[5]
    diag_real = total[None] - mass_shift[:, None, None, None] * density[None]
    diag_imag = LOSS_FACTOR * total
    angles = 2.0 * jnp.pi / NSECT * harmonic.astype(jnp.float32)
    cosines = jnp.cos(angles)
    sines = jnp.sin(angles)
    solution = jnp.zeros_like(rhs)
    residual = rhs
    for iteration in range(ITERS):
        if iteration > 0:
            residual = rhs - operate(solution, weights, diag_real, diag_imag, cosines, sines)
        correction = coarse_correction(residual, radial_factor, axial_factor)
        solution = solution + jacobi_step(residual, diag_real, diag_imag) + correction
    residual = rhs - operate(solution, weights, diag_real, diag_imag, cosines, sines)
    return (solution, residual)


def solution(mesh):
    return jax.shard_map(
        local,
        mesh=mesh,
        in_specs=(
            P(None, None, None, "radial", "axial"),
            P(None, "radial", "axial"),
            P(),
            P(),
            P(),
            P(),
            P(),
            P(),
        ),
        out_specs=(P(None, None, None, "radial", "axial"), P(None, None, None, "radial", "axial")),
        check_vma=False,
    )
```

profile of v0, /device:TPU:12, one launch (start us, length us, event | category | flops | bytes accessed | tf_op | source)
XLA Modules:
  0.0 395.2 jit_solution(4183586601979156998)
XLA Ops:
  0.6 1.5 fusion.101
  2.1 1.5 fusion.100
  3.6 4.6 %select_add_fusion = (f32[96,8,128]{2,0,1:T(8,128)}, pred[96,8,128]{2,0,1:T(8,128)(4,1)S(1)}, pred[96,8,128]{2,0,1:T(8,128)(4,1)S(1)}, pred[96,8,128]{2,0,1:T(8,128)(4,1)S(1)}, pred[96,8,128]{2,0,1:T(8,128)(4,1)S(1)}) fusion(f32[]{:T(128)} %bitcast.7, f32[]{:T(128)} %bitcast.6, f32[]{:T(128)} %bitcast.5, f32[]{:T(128)} %bitcast.4, s32[96,8,128]{2,1,0:T(8,128)} %param.9), kind=kLoop, calls=%fused_computation.139 | loop fusion | flops 1081344 | bytes 1179664 | tf_op jit(solution)/shard_map/add | solution.py:30
  8.2 2.8 select_add_fusion.1
  11.1 1.9 collective-permute-start.1
  13.0 4.5 %collective-permute-start = (f32[96,1,128]{2,0,1:T(8,128)S(1)}, f32[96,1,128]{2,0,1:T(8,128)S(1)}, u32[]{:S(2)}, u32[]{:S(2)}) collective-permute-start(f32[96,1,128]{2,0,1:T(8,128)S(1)} %get-tuple-element.85), channel_id=1, source_target_pairs={{4,0},{8,4},{12,8},{16,12},{20,16},{24,20},{28,24},{5,1},{9,5},{13... | collective-permute-start | bytes 147464 | tf_op jit(solution)/shard_map/ppermute | solution.py:22
  18.9 65.0 %all-gather = f32[64,2,2,16]{3,2,1,0:T(2,128)S(1)} all-gather(f32[2,2,2,16]{3,2,1,0:T(2,128)S(1)} %reduce_sum.38), channel_id=2, replica_groups=mesh['radial'=8,'axial'=4] {'radial','axial'}, dimensions={0}, use_global_device_ids=true | all-gather | bytes 16896 | tf_op jit(solution)/shard_map/all_gather | solution.py:128
  89.5 4.8 %collective-permute-start.2 = (f32[96,10,1]{0,1,2:T(8,128)S(1)}, f32[96,10,1]{0,1,2:T(8,128)S(1)}, u32[]{:S(2)}, u32[]{:S(2)}) collective-permute-start(f32[96,10,1]{0,1,2:T(8,128)S(1)} %copy.253), channel_id=1, source_target_pairs={{1,0},{2,1},{3,2},{5,4},{6,5},{7,6},{9,8},{10,9},{11,10},{13,12},{... | collective-permute-start | bytes 11528 | tf_op jit(solution)/shard_map/ppermute | solution.py:22
  94.5 1.9 collective-permute-start.3
  96.5 1.2 copy.213
  98.2 1.9 collective-permute-done.3
  101.1 2.9 broadcast_multiply_fusion
  107.0 1.9 collective-permute-start.4
  109.0 2.4 collective-permute-start.5
  111.4 1.1 fusion.91
  115.4 1.5 collective-permute-done.5
  118.1 3.6 fusion.83
  121.7 2.4 copy.225
  124.1 1.9 collective-permute-start.7
  126.0 3.0 copy.222
  129.0 4.2 %collective-permute-start.6 = (f32[2,2,96,10,1]{2,1,4,3,0:T(2,128)}, f32[2,2,96,10,1]{2,1,4,3,0:T(2,128)}, u32[]{:S(2)}, u32[]{:S(2)}) collective-permute-start(f32[2,2,96,10,1]{2,1,4,3,0:T(2,128)} %copy.222), channel_id=1, source_target_pairs={{1,0},{2,1},{3,2},{5,4},{6,5},{7,6},{9,8},{10,9},{11,10},{13,12},{... | collective-permute-start | bytes 46088 | tf_op jit(solution)/shard_map/ppermute | solution.py:22
  133.2 2.1 maximum_bitcast_fusion.2
  136.3 1.0 copy.227
  141.2 2.4 copy.226
  143.6 3.1 copy.223
  146.7 6.0 %fusion.21 = f32[2,2,96,8,128]{4,3,2,1,0:T(8,128)S(1)} fusion(f32[2,2,96,10,1]{4,3,2,1,0:T(8,128)} %copy.226, f32[2,2,96,1,128]{4,3,2,1,0:T(1,128)S(1)} %collective-permute-done.4, f32[2,2,96,8,128]{4,3,2,1,0:T(8,128)S(1)} %maximum_add_fusion, f32[2,2,96,1,128]{4,3,2,1,0:T(1,128)} %copy-done.32, f32[2,2,96,10,1]{4,3,2,1,0:T(8,128)} %copy.223, ...), kind=kLoop, calls=%fused_computation.41 | loop fusion | flops 8257536 | bytes 9074688 | tf_op jit(solution)/shard_map/add | solution.py:70
  153.2 1.3 fusion.74
  154.6 1.3 copy.249
  155.9 1.4 reduce_sum.44
  157.4 64.0 %all-gather.1 = f32[64,2,2,16]{3,2,1,0:T(2,128)S(1)} all-gather(f32[2,2,2,16]{3,2,1,0:T(2,128)S(1)} %copy.250), channel_id=3, replica_groups=mesh['radial'=8,'axial'=4] {'radial','axial'}, dimensions={0}, use_global_device_ids=true | all-gather | bytes 16896 | tf_op jit(solution)/shard_map/all_gather | solution.py:128
  221.9 3.0 add_multiply_fusion.1
  229.0 2.0 fusion.27
  231.6 1.0 fusion.89
  232.6 1.9 collective-permute-start.8
  234.5 2.4 collective-permute-start.9
  239.7 2.7 collective-permute-done.9
  243.6 3.6 fusion.82
  247.3 2.4 copy.236
  249.6 1.9 collective-permute-start.11
  251.5 3.0 copy.234
  254.5 4.1 %collective-permute-start.10 = (f32[2,2,96,10,1]{2,1,4,3,0:T(2,128)}, f32[2,2,96,10,1]{2,1,4,3,0:T(2,128)}, u32[]{:S(2)}, u32[]{:S(2)}) collective-permute-start(f32[2,2,96,10,1]{2,1,4,3,0:T(2,128)} %copy.234), channel_id=1, source_target_pairs={{1,0},{2,1},{3,2},{5,4},{6,5},{7,6},{9,8},{10,9},{11,10},{13,12},{... | collective-permute-start | bytes 46088 | tf_op jit(solution)/shard_map/ppermute | solution.py:22
  258.6 2.1 maximum_bitcast_fusion.6
  260.7 2.4 copy.237
  263.1 3.1 copy.235
  266.2 6.0 %fusion.12 = f32[2,2,96,8,128]{4,3,2,1,0:T(8,128)S(1)} fusion(f32[2,2,96,10,1]{4,3,2,1,0:T(8,128)} %copy.237, f32[2,2,96,1,128]{4,3,2,1,0:T(1,128)S(1)} %collective-permute-done.8, f32[2,2,96,8,128]{4,3,2,1,0:T(8,128)S(1)} %fusion.27, f32[2,2,96,1,128]{4,3,2,1,0:T(1,128)} %copy-done.34, f32[2,2,96,10,1]{4,3,2,1,0:T(8,128)} %copy.235, ...), kind=kLoop, calls=%fused_computation.24 | loop fusion | flops 8257536 | bytes 9074688 | tf_op jit(solution)/shard_map/add | solution.py:70
  272.7 1.3 fusion.73
  274.1 1.3 copy.251
  275.4 1.4 reduce_sum.56
  276.9 64.0 %all-gather.2 = f32[64,2,2,16]{3,2,1,0:T(2,128)S(1)} all-gather(f32[2,2,2,16]{3,2,1,0:T(2,128)S(1)} %copy.252), channel_id=4, replica_groups=mesh['radial'=8,'axial'=4] {'radial','axial'}, dimensions={0}, use_global_device_ids=true | all-gather | bytes 16896 | tf_op jit(solution)/shard_map/all_gather | solution.py:128
  341.4 3.0 add_multiply_fusion
  348.5 2.6 fusion.28
  353.2 1.9 collective-permute-start.12
  355.1 2.4 collective-permute-start.13
  360.4 2.6 collective-permute-done.13
  364.3 3.6 fusion.81
  367.9 2.6 copy.245
  370.5 1.9 collective-permute-start.15
  372.4 3.2 copy.243
  375.6 4.2 %collective-permute-start.14 = (f32[2,2,96,10,1]{2,3,4,1,0:T(8,128)}, f32[2,2,96,10,1]{2,3,4,1,0:T(8,128)}, u32[]{:S(2)}, u32[]{:S(2)}) collective-permute-start(f32[2,2,96,10,1]{2,3,4,1,0:T(8,128)} %copy.243), channel_id=1, source_target_pairs={{1,0},{2,1},{3,2},{5,4},{6,5},{7,6},{9,8},{10,9},{11,10},{13,12},{... | collective-permute-start | bytes 46088 | tf_op jit(solution)/shard_map/ppermute | solution.py:22
  379.8 2.1 maximum_bitcast_fusion.10
  381.8 2.4 copy.246
  384.2 3.1 copy.244
  387.3 6.0 %fusion.3 = f32[2,2,96,8,128]{4,3,2,1,0:T(8,128)S(1)} fusion(f32[2,2,96,10,1]{4,3,2,1,0:T(8,128)} %copy.246, f32[2,2,96,1,128]{4,3,2,1,0:T(1,128)S(1)} %collective-permute-done.12, f32[2,2,96,8,128]{4,3,2,1,0:T(8,128)S(1)} %fusion.28, f32[2,2,96,1,128]{4,3,2,1,0:T(1,128)} %copy-done.33, f32[2,2,96,10,1]{4,3,2,1,0:T(8,128)} %copy.244, ...), kind=kLoop, calls=%fused_computation.7 | loop fusion | flops 8257536 | bytes 9074688 | tf_op jit(solution)/shard_map/add | solution.py:70
  393.9 1.3 maximum_subtract_fusion.2
  (205 shorter events, 42.3 us)
Async XLA Ops:
  0.6 83.5 %copy-start = (f32[2,2,64,64]{3,2,1,0:T(8,128)S(1)}, f32[2,2,64,64]{3,2,1,0:T(8,128)}, u32[]{:S(2)}) copy-start(f32[2,2,64,64]{3,2,1,0:T(8,128)} %param.15) | copy-start | bytes 196612
  8.2 10.3 %copy-start.2 = (f32[2,2,96,8,128]{4,3,2,1,0:T(8,128)S(1)}, f32[2,2,96,8,128]{4,3,2,1,0:T(8,128)}, u32[]{:S(2)}) copy-start(f32[2,2,96,8,128]{4,3,2,1,0:T(8,128)} %param.8) | copy-start | bytes 4718596
  11.1 77.8 %collective-permute-start.1 = (f32[96,1,128]{2,0,1:T(8,128)S(1)}, f32[96,1,128]{2,0,1:T(8,128)S(1)}, u32[]{:S(2)}, u32[]{:S(2)}) collective-permute-start(f32[96,1,128]{2,0,1:T(8,128)S(1)} %get-tuple-element.86), channel_id=1, source_target_pairs={{0,4},{4,8},{8,12},{12,16},{16,20},{20,24},{24,28},{1,5},{5,9},{9,... | collective-permute-start | bytes 147464 | tf_op jit(solution)/shard_map/ppermute | solution.py:21
  13.0 75.9 %collective-permute-start = (f32[96,1,128]{2,0,1:T(8,128)S(1)}, f32[96,1,128]{2,0,1:T(8,128)S(1)}, u32[]{:S(2)}, u32[]{:S(2)}) collective-permute-start(f32[96,1,128]{2,0,1:T(8,128)S(1)} %get-tuple-element.85), channel_id=1, source_target_pairs={{4,0},{8,4},{12,8},{16,12},{20,16},{24,20},{28,24},{5,1},{9,5},{13... | collective-permute-start | bytes 147464 | tf_op jit(solution)/shard_map/ppermute | solution.py:22
  18.5 68.9 %copy-start.42 = (s32[2]{0:T(128)S(1)}, s32[2]{0:T(128)}, u32[]{:S(2)}) copy-start(s32[2]{0:T(128)} %param.13) | copy-start | bytes 28
  88.9 0.6 copy-start.35
  89.5 8.5 %collective-permute-start.2 = (f32[96,10,1]{0,1,2:T(8,128)S(1)}, f32[96,10,1]{0,1,2:T(8,128)S(1)}, u32[]{:S(2)}, u32[]{:S(2)}) collective-permute-start(f32[96,10,1]{0,1,2:T(8,128)S(1)} %copy.253), channel_id=1, source_target_pairs={{1,0},{2,1},{3,2},{5,4},{6,5},{7,6},{9,8},{10,9},{11,10},{13,12},{... | collective-permute-start | bytes 11528 | tf_op jit(solution)/shard_map/ppermute | solution.py:22
  94.5 5.7 %collective-permute-start.3 = (f32[96,10,1]{0,1,2:T(8,128)S(1)}, f32[96,10,1]{0,1,2:T(8,128)}, u32[]{:S(2)}, u32[]{:S(2)}) collective-permute-start(f32[96,10,1]{0,1,2:T(8,128)S(1)} %copy.254), channel_id=1, source_target_pairs={{0,1},{1,2},{2,3},{4,5},{5,6},{6,7},{8,9},{9,10},{10,11},{12,13},{... | collective-permute-start | bytes 11528 | tf_op jit(solution)/shard_map/ppermute | solution.py:21
  97.7 7.0 %copy-start.3 = (f32[96,8,128]{2,1,0:T(8,128)}, f32[96,8,128]{2,1,0:T(8,128)S(1)}, u32[]{:S(2)}) copy-start(f32[96,8,128]{2,1,0:T(8,128)S(1)} %copy.213) | copy-start | bytes 1179652
  103.9 0.8 copy-start.36
  104.2 1.0 copy-start.9
  104.5 0.8 copy-start.23
  104.7 0.8 copy-start.15
  105.5 0.9 copy-start.21
  105.5 1.2 copy-start.22
  107.0 8.4 %collective-permute-start.4 = (f32[2,2,96,1,128]{4,3,2,1,0:T(1,128)S(1)}, f32[2,2,96,1,128]{4,3,2,1,0:T(1,128)S(1)}, u32[]{:S(2)}, u32[]{:S(2)}) collective-permute-start(f32[2,2,96,1,128]{4,3,2,1,0:T(1,128)S(1)} %get-tuple-element.66), channel_id=1, source_target_pairs={{4,0},{8,4},{12,8},{16,12},{20,16},{24,20},{28,24},{5,1},{9,5},{13... | collective-permute-start | bytes 589832 | tf_op jit(solution)/shard_map/ppermute | solution.py:22
  109.0 7.9 %collective-permute-start.5 = (f32[2,2,96,1,128]{4,3,2,1,0:T(1,128)S(1)}, f32[2,2,96,1,128]{4,3,2,1,0:T(1,128)S(1)}, u32[]{:S(2)}, u32[]{:S(2)}) collective-permute-start(f32[2,2,96,1,128]{4,3,2,1,0:T(1,128)S(1)} %get-tuple-element.65), channel_id=1, source_target_pairs={{0,4},{4,8},{8,12},{12,16},{16,20},{20,24},{24,28},{1,5},{5,9},{9,... | collective-permute-start | bytes 589832 | tf_op jit(solution)/shard_map/ppermute | solution.py:21
  111.4 1.1 copy-start.38
  111.4 1.1 copy-start.40
  116.9 0.7 copy-start.32
  124.1 17.2 %collective-permute-start.7 = (f32[2,2,96,10,1]{2,1,4,3,0:T(2,128)S(1)}, f32[2,2,96,10,1]{2,1,4,3,0:T(2,128)S(1)}, u32[]{:S(2)}, u32[]{:S(2)}) collective-permute-start(f32[2,2,96,10,1]{2,1,4,3,0:T(2,128)S(1)} %copy.225), channel_id=1, source_target_pairs={{0,1},{1,2},{2,3},{4,5},{5,6},{6,7},{8,9},{9,10},{10,11},{12,13},{... | collective-permute-start | bytes 46088 | tf_op jit(solution)/shard_map/ppermute | solution.py:21
  129.0 6.4 %copy-start.31 = (f32[96,8,128]{2,0,1:T(8,128)S(1)}, f32[96,8,128]{2,0,1:T(8,128)}, u32[]{:S(2)}) copy-start(f32[96,8,128]{2,0,1:T(8,128)} %get-tuple-element.24) | copy-start | bytes 1179652
  129.0 7.3 %copy-start.30 = (f32[96,8,128]{2,0,1:T(8,128)S(1)}, f32[96,8,128]{2,0,1:T(8,128)}, u32[]{:S(2)}) copy-start(f32[96,8,128]{2,0,1:T(8,128)} %get-tuple-element.23) | copy-start | bytes 1179652
  129.0 14.7 %collective-permute-start.6 = (f32[2,2,96,10,1]{2,1,4,3,0:T(2,128)}, f32[2,2,96,10,1]{2,1,4,3,0:T(2,128)}, u32[]{:S(2)}, u32[]{:S(2)}) collective-permute-start(f32[2,2,96,10,1]{2,1,4,3,0:T(2,128)} %copy.222), channel_id=1, source_target_pairs={{1,0},{2,1},{3,2},{5,4},{6,5},{7,6},{9,8},{10,9},{11,10},{13,12},{... | collective-permute-start | bytes 46088 | tf_op jit(solution)/shard_map/ppermute | solution.py:22
  133.2 4.1 %copy-start.29 = (f32[96,8,128]{2,0,1:T(8,128)S(1)}, f32[96,8,128]{2,0,1:T(8,128)}, u32[]{:S(2)}) copy-start(f32[96,8,128]{2,0,1:T(8,128)} %get-tuple-element.22) | copy-start | bytes 1179652
  135.3 3.0 copy-start.28
  135.3 4.0 %copy-start.27 = (f32[96,8,128]{2,0,1:T(8,128)S(1)}, f32[96,8,128]{2,0,1:T(8,128)}, u32[]{:S(2)}) copy-start(f32[96,8,128]{2,0,1:T(8,128)} %get-tuple-element.19) | copy-start | bytes 1179652
  136.3 4.0 %copy-start.26 = (f32[96,8,128]{2,0,1:T(8,128)S(1)}, f32[96,8,128]{2,0,1:T(8,128)}, u32[]{:S(2)}) copy-start(f32[96,8,128]{2,0,1:T(8,128)} %get-tuple-element.20) | copy-start | bytes 1179652
  146.7 6.0 %copy-start.4 = (f32[96,8,128]{2,1,0:T(8,128)S(1)}, f32[96,8,128]{2,1,0:T(8,128)}, u32[]{:S(2)}) copy-start(f32[96,8,128]{2,1,0:T(8,128)} %copy-done.3) | copy-start | bytes 1179652
  146.7 6.0 %copy-start.10 = (f32[96,8,128]{2,1,0:T(8,128)S(1)}, f32[96,8,128]{2,1,0:T(8,128)}, u32[]{:S(2)}) copy-start(f32[96,8,128]{2,1,0:T(8,128)} %copy-done.9) | copy-start | bytes 1179652
  146.7 6.0 %copy-start.16 = (f32[96,8,128]{2,1,0:T(8,128)S(1)}, f32[96,8,128]{2,1,0:T(8,128)}, u32[]{:S(2)}) copy-start(f32[96,8,128]{2,1,0:T(8,128)} %copy-done.15) | copy-start | bytes 1179652
  154.6 67.3 %copy-start.5 = (f32[96,8,128]{2,1,0:T(8,128)S(1)}, f32[96,8,128]{2,1,0:T(8,128)}, u32[]{:S(2)}) copy-start(f32[96,8,128]{2,1,0:T(8,128)} %copy-done.3) | copy-start | bytes 1179652
  154.6 67.3 %copy-start.11 = (f32[96,8,128]{2,1,0:T(8,128)S(1)}, f32[96,8,128]{2,1,0:T(8,128)}, u32[]{:S(2)}) copy-start(f32[96,8,128]{2,1,0:T(8,128)} %copy-done.9) | copy-start | bytes 1179652
  154.6 67.3 %copy-start.17 = (f32[96,8,128]{2,1,0:T(8,128)S(1)}, f32[96,8,128]{2,1,0:T(8,128)}, u32[]{:S(2)}) copy-start(f32[96,8,128]{2,1,0:T(8,128)} %copy-done.15) | copy-start | bytes 1179652
  154.6 67.4 %copy-start.24 = (f32[96,8,128]{2,1,0:T(8,128)S(1)}, f32[96,8,128]{2,1,0:T(8,128)}, u32[]{:S(2)}) copy-start(f32[96,8,128]{2,1,0:T(8,128)} %copy-done.23) | copy-start | bytes 1179652
  232.6 7.1 %collective-permute-start.8 = (f32[2,2,96,1,128]{4,3,2,1,0:T(1,128)S(1)}, f32[2,2,96,1,128]{4,3,2,1,0:T(1,128)S(1)}, u32[]{:S(2)}, u32[]{:S(2)}) collective-permute-start(f32[2,2,96,1,128]{4,3,2,1,0:T(1,128)S(1)} %get-tuple-element.62), channel_id=1, source_target_pairs={{4,0},{8,4},{12,8},{16,12},{20,16},{24,20},{28,24},{5,1},{9,5},{13... | collective-permute-start | bytes 589832 | tf_op jit(solution)/shard_map/ppermute | solution.py:22
  234.5 7.9 %collective-permute-start.9 = (f32[2,2,96,1,128]{4,3,2,1,0:T(1,128)S(1)}, f32[2,2,96,1,128]{4,3,2,1,0:T(1,128)S(1)}, u32[]{:S(2)}, u32[]{:S(2)}) collective-permute-start(f32[2,2,96,1,128]{4,3,2,1,0:T(1,128)S(1)} %get-tuple-element.61), channel_id=1, source_target_pairs={{0,4},{4,8},{8,12},{12,16},{16,20},{20,24},{24,28},{1,5},{5,9},{9,... | collective-permute-start | bytes 589832 | tf_op jit(solution)/shard_map/ppermute | solution.py:21
  242.4 0.7 copy-start.34
  249.6 11.1 %collective-permute-start.11 = (f32[2,2,96,10,1]{2,1,4,3,0:T(2,128)S(1)}, f32[2,2,96,10,1]{2,1,4,3,0:T(2,128)S(1)}, u32[]{:S(2)}, u32[]{:S(2)}) collective-permute-start(f32[2,2,96,10,1]{2,1,4,3,0:T(2,128)S(1)} %copy.236), channel_id=1, source_target_pairs={{0,1},{1,2},{2,3},{4,5},{5,6},{6,7},{8,9},{9,10},{10,11},{12,13},{... | collective-permute-start | bytes 46088 | tf_op jit(solution)/shard_map/ppermute | solution.py:21
  254.5 8.6 %collective-permute-start.10 = (f32[2,2,96,10,1]{2,1,4,3,0:T(2,128)}, f32[2,2,96,10,1]{2,1,4,3,0:T(2,128)}, u32[]{:S(2)}, u32[]{:S(2)}) collective-permute-start(f32[2,2,96,10,1]{2,1,4,3,0:T(2,128)} %copy.234), channel_id=1, source_target_pairs={{1,0},{2,1},{3,2},{5,4},{6,5},{7,6},{9,8},{10,9},{11,10},{13,12},{... | collective-permute-start | bytes 46088 | tf_op jit(solution)/shard_map/ppermute | solution.py:22
  266.1 6.0 %copy-start.6 = (f32[96,8,128]{2,1,0:T(8,128)S(1)}, f32[96,8,128]{2,1,0:T(8,128)}, u32[]{:S(2)}) copy-start(f32[96,8,128]{2,1,0:T(8,128)} %copy-done.3) | copy-start | bytes 1179652
  266.2 6.0 %copy-start.12 = (f32[96,8,128]{2,1,0:T(8,128)S(1)}, f32[96,8,128]{2,1,0:T(8,128)}, u32[]{:S(2)}) copy-start(f32[96,8,128]{2,1,0:T(8,128)} %copy-done.9) | copy-start | bytes 1179652
  266.2 6.0 %copy-start.18 = (f32[96,8,128]{2,1,0:T(8,128)S(1)}, f32[96,8,128]{2,1,0:T(8,128)}, u32[]{:S(2)}) copy-start(f32[96,8,128]{2,1,0:T(8,128)} %copy-done.15) | copy-start | bytes 1179652
  266.2 6.0 %copy-start.37 = (f32[2]{0:T(128)S(1)}, f32[2]{0:T(128)}, u32[]{:S(2)}) copy-start(f32[2]{0:T(128)} %param.12) | copy-start | bytes 28
  274.0 67.3 %copy-start.7 = (f32[96,8,128]{2,1,0:T(8,128)S(1)}, f32[96,8,128]{2,1,0:T(8,128)}, u32[]{:S(2)}) copy-start(f32[96,8,128]{2,1,0:T(8,128)} %copy-done.3) | copy-start | bytes 1179652
  274.0 67.3 %copy-start.13 = (f32[96,8,128]{2,1,0:T(8,128)S(1)}, f32[96,8,128]{2,1,0:T(8,128)}, u32[]{:S(2)}) copy-start(f32[96,8,128]{2,1,0:T(8,128)} %copy-done.9) | copy-start | bytes 1179652
  274.0 67.3 %copy-start.19 = (f32[96,8,128]{2,1,0:T(8,128)S(1)}, f32[96,8,128]{2,1,0:T(8,128)}, u32[]{:S(2)}) copy-start(f32[96,8,128]{2,1,0:T(8,128)} %copy-done.15) | copy-start | bytes 1179652
  274.0 67.4 %copy-start.25 = (f32[96,8,128]{2,1,0:T(8,128)S(1)}, f32[96,8,128]{2,1,0:T(8,128)}, u32[]{:S(2)}) copy-start(f32[96,8,128]{2,1,0:T(8,128)} %copy-done.23) | copy-start | bytes 1179652
  351.1 42.2 %copy-start.1 = (f32[2,2,96,8,128]{4,3,2,1,0:T(8,128)}, f32[2,2,96,8,128]{4,3,2,1,0:T(8,128)S(1)}, u32[]{:S(2)}) copy-start(f32[2,2,96,8,128]{4,3,2,1,0:T(8,128)S(1)} %fusion.28) | copy-start | bytes 4718596
  351.5 0.6 copy-start.39
  351.5 0.7 copy-start.41
  353.2 7.2 %collective-permute-start.12 = (f32[2,2,96,1,128]{4,3,2,1,0:T(1,128)S(1)}, f32[2,2,96,1,128]{4,3,2,1,0:T(1,128)S(1)}, u32[]{:S(2)}, u32[]{:S(2)}) collective-permute-start(f32[2,2,96,1,128]{4,3,2,1,0:T(1,128)S(1)} %get-tuple-element.58), channel_id=1, source_target_pairs={{4,0},{8,4},{12,8},{16,12},{20,16},{24,20},{28,24},{5,1},{9,5},{13... | collective-permute-start | bytes 589832 | tf_op jit(solution)/shard_map/ppermute | solution.py:22
  355.1 7.9 %collective-permute-start.13 = (f32[2,2,96,1,128]{4,3,2,1,0:T(1,128)S(1)}, f32[2,2,96,1,128]{4,3,2,1,0:T(1,128)S(1)}, u32[]{:S(2)}, u32[]{:S(2)}) collective-permute-start(f32[2,2,96,1,128]{4,3,2,1,0:T(1,128)S(1)} %get-tuple-element.57), channel_id=1, source_target_pairs={{0,4},{4,8},{8,12},{12,16},{16,20},{20,24},{24,28},{1,5},{5,9},{9,... | collective-permute-start | bytes 589832 | tf_op jit(solution)/shard_map/ppermute | solution.py:21
  363.0 0.7 copy-start.33
  370.5 11.4 %collective-permute-start.15 = (f32[2,2,96,10,1]{2,3,4,1,0:T(8,128)S(1)}, f32[2,2,96,10,1]{2,3,4,1,0:T(8,128)S(1)}, u32[]{:S(2)}, u32[]{:S(2)}) collective-permute-start(f32[2,2,96,10,1]{2,3,4,1,0:T(8,128)S(1)} %copy.245), channel_id=1, source_target_pairs={{0,1},{1,2},{2,3},{4,5},{5,6},{6,7},{8,9},{9,10},{10,11},{12,13},{... | collective-permute-start | bytes 46088 | tf_op jit(solution)/shard_map/ppermute | solution.py:21
  375.6 8.7 %collective-permute-start.14 = (f32[2,2,96,10,1]{2,3,4,1,0:T(8,128)}, f32[2,2,96,10,1]{2,3,4,1,0:T(8,128)}, u32[]{:S(2)}, u32[]{:S(2)}) collective-permute-start(f32[2,2,96,10,1]{2,3,4,1,0:T(8,128)} %copy.243), channel_id=1, source_target_pairs={{1,0},{2,1},{3,2},{5,4},{6,5},{7,6},{9,8},{10,9},{11,10},{13,12},{... | collective-permute-start | bytes 46088 | tf_op jit(solution)/shard_map/ppermute | solution.py:22
  387.3 6.0 %copy-start.8 = (f32[96,8,128]{2,1,0:T(8,128)S(1)}, f32[96,8,128]{2,1,0:T(8,128)}, u32[]{:S(2)}) copy-start(f32[96,8,128]{2,1,0:T(8,128)} %copy-done.3) | copy-start | bytes 1179652
  387.3 6.0 %copy-start.14 = (f32[96,8,128]{2,1,0:T(8,128)S(1)}, f32[96,8,128]{2,1,0:T(8,128)}, u32[]{:S(2)}) copy-start(f32[96,8,128]{2,1,0:T(8,128)} %copy-done.9) | copy-start | bytes 1179652
  387.3 6.0 %copy-start.20 = (f32[96,8,128]{2,1,0:T(8,128)S(1)}, f32[96,8,128]{2,1,0:T(8,128)}, u32[]{:S(2)}) copy-start(f32[96,8,128]{2,1,0:T(8,128)} %copy-done.15) | copy-start | bytes 1179652
where the time goes:
time: 397 us; the launch traced here: 395 us
  blocking collectives  193 us (49%)
  local copies, waits for them, and re-layouts  70.6 us (18%)
  other arithmetic  65.2 us (16%)
  starting transfers between devices  44.3 us (11%)
  matrix products  11.9 us (3%)
  waiting for transfers between devices  8.7 us (2%)
    all_gather x3, blocking collectives, coarse_correction(): lax.all_gather(coarse_res[None], ('radial', 'axial'), axis=0, tiled=True)  193 us
    ppermute x8, starting transfers between devices, extended(): after = lax.ppermute(first, axis, down)  27.6 us
    slice x7, local copies, waits for them, and re-layouts, extended(): first = lax.slice_in_dim(shard, 0, width, axis=dim)  20 us
    add x3, other arithmetic, neighbours(): return summed + weights[4] * ahead + weights[5] * behind  18 us
    ppermute x8, starting transfers between devices, extended(): before = lax.ppermute(last, axis, up)  16.8 us
    dot_general x12, matrix products, matmul(): jnp.einsum('hij,hjk->hik', first, second, precision=lax.Precision.HIGHEST)  10.1 us
    ppermute x4, local copies, waits for them, and re-layouts, extended(): after = lax.ppermute(first, axis, down)  9.47 us
    another operation x6, other arithmetic, neighbours(): jnp.stack([jnp.concatenate([back_real, real_part[:, :-1]], 1), jnp.concat...  9.15 us
  transfers between devices with their start and end apart: 16, of which 4 were waited for; matrix products, arithmetic and copies ran while one was open for 12% of the time, Pallas kernels for 0%

commit v1 on v0

--- a/solution.py
+++ b/solution.py
@@ -1,7 +1,9 @@
+import functools
 import jax
 import jax.numpy as jnp
 from jax import lax
 from jax.sharding import PartitionSpec as P
+from jax.lax import axis_index, axis_size, ppermute
 
 ITERS = 3
 NSECT = 24
@@ -9,6 +11,21 @@
 AA = 8
 LOSS_FACTOR = 0.2
 RELAXATION = 0.6
+
+
+def start_lots_all(x_part, net_axis):
+    passed, r2 = (axis_size(net_axis), axis_index(net_axis))
+    carry_out, big = (x_part, 1)
+    while big < passed:
+        met_up = ppermute(carry_out, net_axis, [(dd, dd ^ big) for dd in range(passed)])
+        block_out = jnp.concatenate([carry_out, met_up], axis=0)
+        q_next = jnp.concatenate([met_up, carry_out], 0)
+        carry_out = jnp.where(r2 & big == 0, block_out, q_next)
+        big = 2 * big
+    return carry_out
+
+
+carry_flows_up = functools.partial(start_lots_all, net_axis=("radial", "axial"))
 
 
 def extended(shard, sides, width):
@@ -125,7 +142,7 @@
     )
     radial_count = lax.axis_size("radial")
     axial_count = lax.axis_size("axial")
-    collected = lax.all_gather(coarse_res[None], ("radial", "axial"), axis=0, tiled=True)
+    collected = carry_flows_up(coarse_res[None])
     collected = collected.reshape(radial_count, axial_count, 2, shape[1], band_rows, band_cols)
     collected = collected.transpose(2, 3, 0, 4, 1, 5).reshape(
         2, shape[1], radial_count * band_rows, axial_count * band_cols

time: 397 us -> 240 us (0.60)
  blocking collectives: 193 us -> 0 us
  waiting for transfers between devices: 8.7 us -> 44.8 us
  starting transfers between devices: 44.3 us -> 49.9 us
    all_gather x3 -> x0, blocking collectives: 193 us -> none  [coarse_correction(): lax.all_gather(coarse_res[None], ('radial', 'axial'), axis=0, tiled=True)]
    ppermute x0 -> x15, waiting for transfers between devices: none -> 35.5 us  [start_lots_all(): ppermute(carry_out, net_axis, [(dd, dd ^ big) for dd in range(passed)])]
    ppermute x0 -> x15, starting transfers between devices: none -> 6.35 us  [start_lots_all(): ppermute(carry_out, net_axis, [(dd, dd ^ big) for dd in range(passed)])]
    unnamed x92 -> x96, local copies, waits for them, and re-layouts: 7.64 us -> 8.44 us
  transfers between devices with their start and end apart: 16 -> 31, of which waited for: 4 -> 17; matrix products, arithmetic and copies ran while one was open for 12% -> 24% of each run, Pallas kernels for 0% -> 0%
where the time goes in v1:
time: 240 us; the launch traced here: 239 us
  local copies, waits for them, and re-layouts  66.8 us (28%)
  other arithmetic  63.7 us (27%)
  starting transfers between devices  49.9 us (21%)
  waiting for transfers between devices  44.8 us (19%)
  matrix products  11.9 us (5%)
    ppermute x15, waiting for transfers between devices, start_lots_all(): ppermute(carry_out, net_axis, [(dd, dd ^ big) for dd in range(passed)])  35.5 us
    ppermute x8, starting transfers between devices, extended(): after = lax.ppermute(first, axis, down)  25 us
    slice x7, local copies, waits for them, and re-layouts, extended(): first = lax.slice_in_dim(shard, 0, width, axis=dim)  19.9 us
    ppermute x8, starting transfers between devices, extended(): before = lax.ppermute(last, axis, up)  18.5 us
    add x3, other arithmetic, neighbours(): return summed + weights[4] * ahead + weights[5] * behind  18.1 us
    dot_general x12, matrix products, matmul(): jnp.einsum('hij,hjk->hik', first, second, precision=lax.Precision.HIGHEST)  10.1 us
    ppermute x4, local copies, waits for them, and re-layouts, extended(): after = lax.ppermute(first, axis, down)  9.38 us
    ppermute x8, waiting for transfers between devices, extended(): before = lax.ppermute(last, axis, up)  9.32 us
  transfers between devices with their start and end apart: 31, of which 17 were waited for; matrix products, arithmetic and copies ran while one was open for 24% of the time, Pallas kernels for 0%

profile of v1, /device:TPU:12, one launch (start us, length us, event | category | flops | bytes accessed | tf_op | source)
XLA Modules:
  0.0 238.8 jit_solution(2384012339527760500)
XLA Ops:
  0.7 1.6 reduce_sum.36
  4.4 2.8 %select_add_fusion = (f32[96,8,128]{2,0,1:T(8,128)S(1)}, pred[96,8,128]{2,0,1:T(8,128)(4,1)S(1)}, pred[96,8,128]{2,0,1:T(8,128)(4,1)S(1)}, pred[96,8,128]{2,0,1:T(8,128)(4,1)S(1)}, pred[96,8,128]{2,0,1:T(8,128)(4,1)S(1)}) fusion(f32[]{:T(128)} %bitcast.7, f32[]{:T(128)} %bitcast.6, f32[]{:T(128)} %bitcast.5, f32[]{:T(128)} %bitcast.4, ...), kind=kLoop, calls=%fused_computation.139 | loop fusion | flops 1081344 | bytes 1179664 | tf_op jit(solution)/shard_map/add | solution.py:47
  7.2 2.7 %select_add_fusion.1 = f32[96,8,128]{2,0,1:T(8,128)S(1)} fusion(pred[96,8,128]{2,0,1:T(8,128)(4,1)S(1)} %get-tuple-element.16, pred[96,8,128]{2,0,1:T(8,128)(4,1)S(1)} %get-tuple-element.15, pred[96,8,128]{2,0,1:T(8,128)(4,1)S(1)} %get-tuple-element.14, pred[96,8,128]{2,0,1:T(8,128)(4,1)S(1)} %get-tuple-element.13, f32[]{:T(128)} %bitcast.3, f32[]{:T(128)} %bitcast.2, ...), kind=kLoop, calls=%fused_computation.141 | loop fusion | flops 688128 | bytes 786448 | tf_op jit(solution)/shard_map/add | solution.py:47
  10.0 2.7 %collective-permute-start.5 = (f32[2,2,2,2,16]{4,3,2,1,0:T(2,128)S(1)}, f32[2,2,2,2,16]{4,3,2,1,0:T(2,128)S(1)}, u32[]{:S(2)}, u32[]{:S(2)}) collective-permute-start(f32[2,2,2,2,16]{4,3,2,1,0:T(2,128)S(1)} %maximum_select_fusion.12), channel_id=1, source_target_pairs={{0,2},{1,3},{2,0},{3,1},{4,6},{5,7},{6,4},{7,5},{8,10},{9,11},{10,... | collective-permute-start | bytes 3080 | tf_op jit(solution)/shard_map/ppermute | solution.py:20
  12.6 1.9 collective-permute-start.1
  14.6 4.5 %collective-permute-start = (f32[96,1,128]{2,0,1:T(8,128)S(1)}, f32[96,1,128]{2,0,1:T(8,128)S(1)}, u32[]{:S(2)}, u32[]{:S(2)}) collective-permute-start(f32[96,1,128]{2,0,1:T(8,128)S(1)} %get-tuple-element.85), channel_id=1, source_target_pairs={{4,0},{8,4},{12,8},{16,12},{20,16},{24,20},{28,24},{5,1},{9,5},{13... | collective-permute-start | bytes 147464 | tf_op jit(solution)/shard_map/ppermute | solution.py:39
  21.1 3.3 %collective-permute-done.7 = f32[8,2,2,2,16]{4,3,2,1,0:T(2,128)S(1)} collective-permute-done((f32[8,2,2,2,16]{4,3,2,1,0:T(2,128)S(1)}, f32[8,2,2,2,16]{4,3,2,1,0:T(2,128)S(1)}, u32[]{:S(2)}, u32[]{:S(2)}) %collective-permute-start.7) | collective-permute-done | bytes 4128 | tf_op jit(solution)/shard_map/ppermute | solution.py:20
  24.9 3.9 %collective-permute-done.8 = f32[16,2,2,2,16]{4,3,2,1,0:T(2,128)S(1)} collective-permute-done((f32[16,2,2,2,16]{4,3,2,1,0:T(2,128)S(1)}, f32[16,2,2,2,16]{4,3,2,1,0:T(2,128)S(1)}, u32[]{:S(2)}, u32[]{:S(2)}) %collective-permute-start.8) | collective-permute-done | bytes 8224 | tf_op jit(solution)/shard_map/ppermute | solution.py:20
  33.6 3.5 %collective-permute-start.2 = (f32[96,10,1]{0,1,2:T(8,128)S(1)}, f32[96,10,1]{0,1,2:T(8,128)S(1)}, u32[]{:S(2)}, u32[]{:S(2)}) collective-permute-start(f32[96,10,1]{0,1,2:T(8,128)S(1)} %copy.223), channel_id=1, source_target_pairs={{1,0},{2,1},{3,2},{5,4},{6,5},{7,6},{9,8},{10,9},{11,10},{13,12},{... | collective-permute-start | bytes 11528 | tf_op jit(solution)/shard_map/ppermute | solution.py:39
  37.4 2.4 collective-permute-start.3
  40.3 2.6 %collective-permute-done.3 = f32[96,10,1]{0,1,2:T(8,128)S(1)} collective-permute-done((f32[96,10,1]{0,1,2:T(8,128)S(1)}, f32[96,10,1]{0,1,2:T(8,128)S(1)}, u32[]{:S(2)}, u32[]{:S(2)}) %collective-permute-start.3) | collective-permute-done | bytes 3872 | tf_op jit(solution)/shard_map/ppermute | solution.py:38
  43.2 1.7 broadcast_multiply_fusion
  48.9 1.9 collective-permute-start.9
  50.8 2.4 %collective-permute-start.10 = (f32[2,2,96,1,128]{4,3,2,1,0:T(1,128)S(1)}, f32[2,2,96,1,128]{4,3,2,1,0:T(1,128)S(1)}, u32[]{:S(2)}, u32[]{:S(2)}) collective-permute-start(f32[2,2,96,1,128]{4,3,2,1,0:T(1,128)S(1)} %get-tuple-element.65), channel_id=1, source_target_pairs={{0,4},{4,8},{8,12},{12,16},{16,20},{20,24},{24,28},{1,5},{5,9},{9,... | collective-permute-start | bytes 589832 | tf_op jit(solution)/shard_map/ppermute | solution.py:38
  57.2 1.5 collective-permute-done.10
  59.9 3.6 %fusion.83 = (f32[2,2,96,10,1]{4,3,2,1,0:T(8,128)}, f32[2,2,96,10,1]{4,3,2,1,0:T(8,128)}) fusion(f32[2,2,96,10,128]{4,3,2,1,0:T(8,128)S(1)} %pad_maximum_fusion), kind=kLoop, calls=%fused_computation.216 | loop fusion | bytes 61440 | tf_op jit(solution)/shard_map/slice | solution.py:37
  63.5 2.4 copy.199
  65.9 2.3 collective-permute-start.12
  68.2 2.9 %copy.196 = f32[2,2,96,10,1]{2,1,4,3,0:T(2,128)} copy(f32[2,2,96,10,1]{4,3,2,1,0:T(8,128)} %get-tuple-element.41) | data formatting | bytes 30720 | tf_op jit(solution)/shard_map/slice | solution.py:37
  71.2 3.8 %collective-permute-start.11 = (f32[2,2,96,10,1]{2,1,4,3,0:T(2,128)}, f32[2,2,96,10,1]{2,1,4,3,0:T(2,128)}, u32[]{:S(2)}, u32[]{:S(2)}) collective-permute-start(f32[2,2,96,10,1]{2,1,4,3,0:T(2,128)} %copy.196), channel_id=1, source_target_pairs={{1,0},{2,1},{3,2},{5,4},{6,5},{7,6},{9,8},{10,9},{11,10},{13,12},{... | collective-permute-start | bytes 46088 | tf_op jit(solution)/shard_map/ppermute | solution.py:39
  75.0 2.2 maximum_bitcast_fusion.2
  83.1 2.3 copy.200
  85.5 3.0 %copy.197 = f32[2,2,96,10,1]{4,3,2,1,0:T(8,128)} copy(f32[2,2,96,10,1]{2,1,4,3,0:T(2,128)} %collective-permute-done.11) | data formatting | bytes 30720 | tf_op jit(solution)/shard_map/ppermute | solution.py:39
  88.5 6.0 %fusion.21 = f32[2,2,96,8,128]{4,3,2,1,0:T(8,128)S(1)} fusion(f32[2,2,96,10,1]{4,3,2,1,0:T(8,128)} %copy.200, f32[2,2,96,1,128]{4,3,2,1,0:T(1,128)S(1)} %collective-permute-done.9, f32[2,2,96,8,128]{4,3,2,1,0:T(8,128)S(1)} %maximum_add_fusion, f32[2,2,96,1,128]{4,3,2,1,0:T(1,128)} %copy-done.32, f32[2,2,96,10,1]{4,3,2,1,0:T(8,128)} %copy.197, ...), kind=kLoop, calls=%fused_computation.41 | loop fusion | flops 8257536 | bytes 9074688 | tf_op jit(solution)/shard_map/add | solution.py:87
  95.0 1.3 fusion.74
  96.4 1.3 copy.219
  97.7 1.4 reduce_sum.44
  99.2 3.6 %collective-permute-done.13 = f32[1,2,2,2,16]{4,3,2,1,0:T(2,128)S(1)} collective-permute-done((f32[1,2,2,2,16]{4,3,2,1,0:T(2,128)S(1)}, f32[1,2,2,2,16]{4,3,2,1,0:T(2,128)S(1)}, u32[]{:S(2)}, u32[]{:S(2)}) %collective-permute-start.13) | collective-permute-done | bytes 544 | tf_op jit(solution)/shard_map/ppermute | solution.py:20
  103.6 3.8 %collective-permute-done.14 = f32[2,2,2,2,16]{4,3,2,1,0:T(2,128)S(1)} collective-permute-done((f32[2,2,2,2,16]{4,3,2,1,0:T(2,128)S(1)}, f32[2,2,2,2,16]{4,3,2,1,0:T(2,128)S(1)}, u32[]{:S(2)}, u32[]{:S(2)}) %collective-permute-start.14) | collective-permute-done | bytes 1056 | tf_op jit(solution)/shard_map/ppermute | solution.py:20
  108.8 3.9 %collective-permute-done.16 = f32[8,2,2,2,16]{4,3,2,1,0:T(2,128)S(1)} collective-permute-done((f32[8,2,2,2,16]{4,3,2,1,0:T(2,128)S(1)}, f32[8,2,2,2,16]{4,3,2,1,0:T(2,128)S(1)}, u32[]{:S(2)}, u32[]{:S(2)}) %collective-permute-start.16) | collective-permute-done | bytes 4128 | tf_op jit(solution)/shard_map/ppermute | solution.py:20
  112.9 3.0 %add_multiply_fusion.1 = (f32[1,2,96,8,128]{4,3,2,1,0:T(8,128)}, f32[1,2,96,8,128]{4,3,2,1,0:T(8,128)}) fusion(f32[2,2,96,8,128]{4,3,2,1,0:T(8,128)} %get-tuple-element.11, f32[96,8,128]{2,1,0:T(8,128)S(1)} %copy-done.24, f32[96,8,128]{2,1,0:T(8,128)S(1)} %copy-done.17, f32[96,8,128]{2,1,0:T(8,128)S(1)} %copy-done.5, f32[2]{0:T(128)S(1)} %copy-done.36, ...), kind=kLoop, calls=%fused_computation.105 | loop fusion | flops 2555904 | bytes 4718600 | tf_op jit(solution)/shard_map/mul | solution.py:126
  121.7 2.0 fusion.27
  125.3 1.9 collective-permute-start.18
  127.2 2.4 %collective-permute-start.19 = (f32[2,2,96,1,128]{4,3,2,1,0:T(1,128)S(1)}, f32[2,2,96,1,128]{4,3,2,1,0:T(1,128)S(1)}, u32[]{:S(2)}, u32[]{:S(2)}) collective-permute-start(f32[2,2,96,1,128]{4,3,2,1,0:T(1,128)S(1)} %get-tuple-element.61), channel_id=1, source_target_pairs={{0,4},{4,8},{8,12},{12,16},{16,20},{20,24},{24,28},{1,5},{5,9},{9,... | collective-permute-start | bytes 589832 | tf_op jit(solution)/shard_map/ppermute | solution.py:38
  132.4 2.7 %collective-permute-done.19 = f32[2,2,96,1,128]{4,3,2,1,0:T(1,128)S(1)} collective-permute-done((f32[2,2,96,1,128]{4,3,2,1,0:T(1,128)S(1)}, f32[2,2,96,1,128]{4,3,2,1,0:T(1,128)S(1)}, u32[]{:S(2)}, u32[]{:S(2)}) %collective-permute-start.19) | collective-permute-done | bytes 196640 | tf_op jit(solution)/shard_map/ppermute | solution.py:38
  136.4 3.6 %fusion.82 = (f32[2,2,96,10,1]{4,3,2,1,0:T(8,128)}, f32[2,2,96,10,1]{4,3,2,1,0:T(8,128)}) fusion(f32[2,2,96,10,128]{4,3,2,1,0:T(8,128)S(1)} %pad_maximum_fusion.1), kind=kLoop, calls=%fused_computation.215 | loop fusion | bytes 61440 | tf_op jit(solution)/shard_map/slice | solution.py:37
  140.0 2.4 copy.208
  142.3 2.3 collective-permute-start.21
  144.7 3.0 %copy.206 = f32[2,2,96,10,1]{2,1,4,3,0:T(2,128)} copy(f32[2,2,96,10,1]{4,3,2,1,0:T(8,128)} %get-tuple-element.39) | data formatting | bytes 30720 | tf_op jit(solution)/shard_map/slice | solution.py:37
  147.6 3.7 %collective-permute-start.20 = (f32[2,2,96,10,1]{2,1,4,3,0:T(2,128)}, f32[2,2,96,10,1]{2,1,4,3,0:T(2,128)}, u32[]{:S(2)}, u32[]{:S(2)}) collective-permute-start(f32[2,2,96,10,1]{2,1,4,3,0:T(2,128)} %copy.206), channel_id=1, source_target_pairs={{1,0},{2,1},{3,2},{5,4},{6,5},{7,6},{9,8},{10,9},{11,10},{13,12},{... | collective-permute-start | bytes 46088 | tf_op jit(solution)/shard_map/ppermute | solution.py:39
  151.3 2.1 maximum_bitcast_fusion.6
  153.4 2.3 copy.209
  155.7 3.0 %copy.207 = f32[2,2,96,10,1]{4,3,2,1,0:T(8,128)} copy(f32[2,2,96,10,1]{2,1,4,3,0:T(2,128)} %collective-permute-done.20) | data formatting | bytes 30720 | tf_op jit(solution)/shard_map/ppermute | solution.py:39
  158.8 6.0 %fusion.12 = f32[2,2,96,8,128]{4,3,2,1,0:T(8,128)S(1)} fusion(f32[2,2,96,10,1]{4,3,2,1,0:T(8,128)} %copy.209, f32[2,2,96,1,128]{4,3,2,1,0:T(1,128)S(1)} %collective-permute-done.18, f32[2,2,96,8,128]{4,3,2,1,0:T(8,128)S(1)} %fusion.27, f32[2,2,96,1,128]{4,3,2,1,0:T(1,128)} %copy-done.34, f32[2,2,96,10,1]{4,3,2,1,0:T(8,128)} %copy.207, ...), kind=kLoop, calls=%fused_computation.24 | loop fusion | flops 8257536 | bytes 9074688 | tf_op jit(solution)/shard_map/add | solution.py:87
  165.3 1.3 fusion.73
  166.7 1.3 copy.221
  168.0 1.4 reduce_sum.56
  169.5 3.6 %collective-permute-done.22 = f32[1,2,2,2,16]{4,3,2,1,0:T(2,128)S(1)} collective-permute-done((f32[1,2,2,2,16]{4,3,2,1,0:T(2,128)S(1)}, f32[1,2,2,2,16]{4,3,2,1,0:T(2,128)S(1)}, u32[]{:S(2)}, u32[]{:S(2)}) %collective-permute-start.22) | collective-permute-done | bytes 544 | tf_op jit(solution)/shard_map/ppermute | solution.py:20
  174.3 3.5 %collective-permute-done.23 = f32[2,2,2,2,16]{4,3,2,1,0:T(2,128)S(1)} collective-permute-done((f32[2,2,2,2,16]{4,3,2,1,0:T(2,128)S(1)}, f32[2,2,2,2,16]{4,3,2,1,0:T(2,128)S(1)}, u32[]{:S(2)}, u32[]{:S(2)}) %collective-permute-start.23) | collective-permute-done | bytes 1056 | tf_op jit(solution)/shard_map/ppermute | solution.py:20
  179.1 3.9 %collective-permute-done.25 = f32[8,2,2,2,16]{4,3,2,1,0:T(2,128)S(1)} collective-permute-done((f32[8,2,2,2,16]{4,3,2,1,0:T(2,128)S(1)}, f32[8,2,2,2,16]{4,3,2,1,0:T(2,128)S(1)}, u32[]{:S(2)}, u32[]{:S(2)}) %collective-permute-start.25) | collective-permute-done | bytes 4128 | tf_op jit(solution)/shard_map/ppermute | solution.py:20
  183.2 2.9 %add_multiply_fusion = (f32[1,2,96,8,128]{4,3,2,1,0:T(8,128)}, f32[1,2,96,8,128]{4,3,2,1,0:T(8,128)}) fusion(f32[2,2,96,8,128]{4,3,2,1,0:T(8,128)} %get-tuple-element.9, f32[96,8,128]{2,1,0:T(8,128)S(1)} %copy-done.25, f32[96,8,128]{2,1,0:T(8,128)S(1)} %copy-done.19, f32[96,8,128]{2,1,0:T(8,128)S(1)} %copy-done.7, f32[2]{0:T(128)S(1)} %copy-done.37, ...), kind=kLoop, calls=%fused_computation.101 | loop fusion | flops 2555904 | bytes 4718600 | tf_op jit(solution)/shard_map/mul | solution.py:126
  192.0 2.6 %fusion.28 = f32[2,2,96,8,128]{4,3,2,1,0:T(8,128)S(1)} fusion(f32[1,2,96,8,128]{4,3,2,1,0:T(8,128)} %get-tuple-element.32, f32[1,2,96,8,128]{4,3,2,1,0:T(8,128)} %get-tuple-element.31, f32[2,2,8,128]{3,2,1,0:T(8,128)S(1)} %add.304, f32[2,2,8,128]{3,2,1,0:T(8,128)S(1)} %add.288, f32[1,2,96,8,128]{4,3,2,1,0:T(8,128)} %get-tuple-element.34, ...), kind=kLoop, calls=%fused_computation.64 | loop fusion | flops 3145728 | bytes 6340608 | tf_op jit(solution)/shard_map/add | solution.py:173
  196.7 1.9 collective-permute-start.27
  198.6 2.4 %collective-permute-start.28 = (f32[2,2,96,1,128]{4,3,2,1,0:T(1,128)S(1)}, f32[2,2,96,1,128]{4,3,2,1,0:T(1,128)S(1)}, u32[]{:S(2)}, u32[]{:S(2)}) collective-permute-start(f32[2,2,96,1,128]{4,3,2,1,0:T(1,128)S(1)} %get-tuple-element.57), channel_id=1, source_target_pairs={{0,4},{4,8},{8,12},{12,16},{16,20},{20,24},{24,28},{1,5},{5,9},{9,... | collective-permute-start | bytes 589832 | tf_op jit(solution)/shard_map/ppermute | solution.py:38
  204.0 2.5 %collective-permute-done.28 = f32[2,2,96,1,128]{4,3,2,1,0:T(1,128)S(1)} collective-permute-done((f32[2,2,96,1,128]{4,3,2,1,0:T(1,128)S(1)}, f32[2,2,96,1,128]{4,3,2,1,0:T(1,128)S(1)}, u32[]{:S(2)}, u32[]{:S(2)}) %collective-permute-start.28) | collective-permute-done | bytes 196640 | tf_op jit(solution)/shard_map/ppermute | solution.py:38
  207.8 3.6 %fusion.81 = (f32[2,2,96,10,1]{4,3,2,1,0:T(8,128)}, f32[2,2,96,10,1]{4,3,2,1,0:T(8,128)}) fusion(f32[2,2,96,10,128]{4,3,2,1,0:T(8,128)S(1)} %pad_maximum_fusion.2), kind=kLoop, calls=%fused_computation.214 | loop fusion | bytes 61440 | tf_op jit(solution)/shard_map/slice | solution.py:37
  211.4 2.6 %copy.215 = f32[2,2,96,10,1]{2,3,4,1,0:T(8,128)S(1)} copy(f32[2,2,96,10,1]{4,3,2,1,0:T(8,128)} %get-tuple-element.38) | data formatting | bytes 30720 | tf_op jit(solution)/shard_map/slice | solution.py:36
  214.0 2.4 collective-permute-start.30
  216.4 3.2 %copy.213 = f32[2,2,96,10,1]{2,3,4,1,0:T(8,128)} copy(f32[2,2,96,10,1]{4,3,2,1,0:T(8,128)} %get-tuple-element.37) | data formatting | bytes 30720 | tf_op jit(solution)/shard_map/slice | solution.py:37
  219.6 3.7 %collective-permute-start.29 = (f32[2,2,96,10,1]{2,3,4,1,0:T(8,128)}, f32[2,2,96,10,1]{2,3,4,1,0:T(8,128)}, u32[]{:S(2)}, u32[]{:S(2)}) collective-permute-start(f32[2,2,96,10,1]{2,3,4,1,0:T(8,128)} %copy.213), channel_id=1, source_target_pairs={{1,0},{2,1},{3,2},{5,4},{6,5},{7,6},{9,8},{10,9},{11,10},{13,12},{... | collective-permute-start | bytes 46088 | tf_op jit(solution)/shard_map/ppermute | solution.py:39
  223.3 2.1 maximum_bitcast_fusion.10
  225.4 2.4 copy.216
  227.7 3.1 %copy.214 = f32[2,2,96,10,1]{4,3,2,1,0:T(8,128)} copy(f32[2,2,96,10,1]{2,3,4,1,0:T(8,128)} %collective-permute-done.29) | data formatting | bytes 30720 | tf_op jit(solution)/shard_map/ppermute | solution.py:39
  230.8 6.2 %fusion.3 = f32[2,2,96,8,128]{4,3,2,1,0:T(8,128)S(1)} fusion(f32[2,2,96,10,1]{4,3,2,1,0:T(8,128)} %copy.216, f32[2,2,96,1,128]{4,3,2,1,0:T(1,128)S(1)} %collective-permute-done.27, f32[2,2,96,8,128]{4,3,2,1,0:T(8,128)S(1)} %fusion.28, f32[2,2,96,1,128]{4,3,2,1,0:T(1,128)} %copy-done.33, f32[2,2,96,10,1]{4,3,2,1,0:T(8,128)} %copy.214, ...), kind=kLoop, calls=%fused_computation.7 | loop fusion | flops 8257536 | bytes 9074688 | tf_op jit(solution)/shard_map/add | solution.py:87
  (245 shorter events, 56.8 us)
Async XLA Ops:
  0.6 28.4 %copy-start = (f32[2,2,64,64]{3,2,1,0:T(8,128)S(1)}, f32[2,2,64,64]{3,2,1,0:T(8,128)}, u32[]{:S(2)}) copy-start(f32[2,2,64,64]{3,2,1,0:T(8,128)} %param.15) | copy-start | bytes 196612
  0.6 2.4 %copy-start.38 = (f32[4]{0:T(128)S(1)}, f32[4]{0:T(128)}, u32[]{:S(2)}) copy-start(f32[4]{0:T(128)} %param.11) | copy-start | bytes 52
  0.7 3.0 %copy-start.39 = (f32[4]{0:T(128)S(1)}, f32[4]{0:T(128)}, u32[]{:S(2)}) copy-start(f32[4]{0:T(128)} %param.10) | copy-start | bytes 52
  0.7 3.7 %copy-start.35 = (s32[96,8,128]{2,1,0:T(8,128)S(1)}, s32[96,8,128]{2,1,0:T(8,128)}, u32[]{:S(2)}) copy-start(s32[96,8,128]{2,1,0:T(8,128)} %param.9) | copy-start | bytes 1179652
  2.5 7.4 %collective-permute-start.4 = (f32[1,2,2,2,16]{4,3,2,1,0:T(2,128)S(1)}, f32[1,2,2,2,16]{4,3,2,1,0:T(2,128)S(1)}, u32[]{:S(2)}, u32[]{:S(2)}) collective-permute-start(f32[1,2,2,2,16]{4,3,2,1,0:T(2,128)S(1)} %bitcast.151), channel_id=1, source_target_pairs={{0,1},{1,0},{2,3},{3,2},{4,5},{5,4},{6,7},{7,6},{8,9},{9,8},{10,11... | collective-permute-start | bytes 1544 | tf_op jit(solution)/shard_map/ppermute | solution.py:20
  7.2 17.3 %copy-start.44 = (s32[2]{0:T(128)S(1)}, s32[2]{0:T(128)}, u32[]{:S(2)}) copy-start(s32[2]{0:T(128)} %param.13) | copy-start | bytes 28
  10.0 9.1 %collective-permute-start.5 = (f32[2,2,2,2,16]{4,3,2,1,0:T(2,128)S(1)}, f32[2,2,2,2,16]{4,3,2,1,0:T(2,128)S(1)}, u32[]{:S(2)}, u32[]{:S(2)}) collective-permute-start(f32[2,2,2,2,16]{4,3,2,1,0:T(2,128)S(1)} %maximum_select_fusion.12), channel_id=1, source_target_pairs={{0,2},{1,3},{2,0},{3,1},{4,6},{5,7},{6,4},{7,5},{8,10},{9,11},{10,... | collective-permute-start | bytes 3080 | tf_op jit(solution)/shard_map/ppermute | solution.py:20
  12.6 20.5 %collective-permute-start.1 = (f32[96,1,128]{2,0,1:T(8,128)S(1)}, f32[96,1,128]{2,0,1:T(8,128)S(1)}, u32[]{:S(2)}, u32[]{:S(2)}) collective-permute-start(f32[96,1,128]{2,0,1:T(8,128)S(1)} %get-tuple-element.86), channel_id=1, source_target_pairs={{0,4},{4,8},{8,12},{12,16},{16,20},{20,24},{24,28},{1,5},{5,9},{9,... | collective-permute-start | bytes 147464 | tf_op jit(solution)/shard_map/ppermute | solution.py:38
  14.6 18.5 %collective-permute-start = (f32[96,1,128]{2,0,1:T(8,128)S(1)}, f32[96,1,128]{2,0,1:T(8,128)S(1)}, u32[]{:S(2)}, u32[]{:S(2)}) collective-permute-start(f32[96,1,128]{2,0,1:T(8,128)S(1)} %get-tuple-element.85), channel_id=1, source_target_pairs={{4,0},{8,4},{12,8},{16,12},{20,16},{24,20},{28,24},{5,1},{9,5},{13... | collective-permute-start | bytes 147464 | tf_op jit(solution)/shard_map/ppermute | solution.py:39
  19.1 1.2 collective-permute-start.6
  20.4 4.0 %collective-permute-start.7 = (f32[8,2,2,2,16]{4,3,2,1,0:T(2,128)S(1)}, f32[8,2,2,2,16]{4,3,2,1,0:T(2,128)S(1)}, u32[]{:S(2)}, u32[]{:S(2)}) collective-permute-start(f32[8,2,2,2,16]{4,3,2,1,0:T(2,128)S(1)} %maximum_select_fusion.6), channel_id=1, source_target_pairs={{0,8},{1,9},{2,10},{3,11},{4,12},{5,13},{6,14},{7,15},{8,0},{9,1},... | collective-permute-start | bytes 12296 | tf_op jit(solution)/shard_map/ppermute | solution.py:20
  24.4 4.3 %collective-permute-start.8 = (f32[16,2,2,2,16]{4,3,2,1,0:T(2,128)S(1)}, f32[16,2,2,2,16]{4,3,2,1,0:T(2,128)S(1)}, u32[]{:S(2)}, u32[]{:S(2)}) collective-permute-start(f32[16,2,2,2,16]{4,3,2,1,0:T(2,128)S(1)} %maximum_select_fusion.3), channel_id=1, source_target_pairs={{0,16},{1,17},{2,18},{3,19},{4,20},{5,21},{6,22},{7,23},{8,24},{9,... | collective-permute-start | bytes 24584 | tf_op jit(solution)/shard_map/ppermute | solution.py:20
  24.6 99.6 %copy-start.40 = (f32[2]{0:T(128)}, f32[2]{0:T(128)S(1)}, u32[]{:S(2)}) copy-start(f32[2]{0:T(128)S(1)} %get-tuple-element.93) | copy-start | bytes 28
  24.6 99.6 %copy-start.42 = (f32[2]{0:T(128)}, f32[2]{0:T(128)S(1)}, u32[]{:S(2)}) copy-start(f32[2]{0:T(128)S(1)} %get-tuple-element.94) | copy-start | bytes 28
  24.8 20.8 %copy-start.3 = (f32[96,8,128]{2,1,0:T(8,128)}, f32[96,8,128]{2,1,0:T(8,128)S(1)}, u32[]{:S(2)}) copy-start(f32[96,8,128]{2,1,0:T(8,128)S(1)} %copy.189) | copy-start | bytes 1179652
  33.6 6.4 %collective-permute-start.2 = (f32[96,10,1]{0,1,2:T(8,128)S(1)}, f32[96,10,1]{0,1,2:T(8,128)S(1)}, u32[]{:S(2)}, u32[]{:S(2)}) collective-permute-start(f32[96,10,1]{0,1,2:T(8,128)S(1)} %copy.223), channel_id=1, source_target_pairs={{1,0},{2,1},{3,2},{5,4},{6,5},{7,6},{9,8},{10,9},{11,10},{13,12},{... | collective-permute-start | bytes 11528 | tf_op jit(solution)/shard_map/ppermute | solution.py:39
  37.4 5.5 %collective-permute-start.3 = (f32[96,10,1]{0,1,2:T(8,128)S(1)}, f32[96,10,1]{0,1,2:T(8,128)S(1)}, u32[]{:S(2)}, u32[]{:S(2)}) collective-permute-start(f32[96,10,1]{0,1,2:T(8,128)S(1)} %copy.224), channel_id=1, source_target_pairs={{0,1},{1,2},{2,3},{4,5},{5,6},{6,7},{8,9},{9,10},{10,11},{12,13},{... | collective-permute-start | bytes 11528 | tf_op jit(solution)/shard_map/ppermute | solution.py:38
  48.9 8.3 %collective-permute-start.9 = (f32[2,2,96,1,128]{4,3,2,1,0:T(1,128)S(1)}, f32[2,2,96,1,128]{4,3,2,1,0:T(1,128)S(1)}, u32[]{:S(2)}, u32[]{:S(2)}) collective-permute-start(f32[2,2,96,1,128]{4,3,2,1,0:T(1,128)S(1)} %get-tuple-element.66), channel_id=1, source_target_pairs={{4,0},{8,4},{12,8},{16,12},{20,16},{24,20},{28,24},{5,1},{9,5},{13... | collective-permute-start | bytes 589832 | tf_op jit(solution)/shard_map/ppermute | solution.py:39
  50.8 7.9 %collective-permute-start.10 = (f32[2,2,96,1,128]{4,3,2,1,0:T(1,128)S(1)}, f32[2,2,96,1,128]{4,3,2,1,0:T(1,128)S(1)}, u32[]{:S(2)}, u32[]{:S(2)}) collective-permute-start(f32[2,2,96,1,128]{4,3,2,1,0:T(1,128)S(1)} %get-tuple-element.65), channel_id=1, source_target_pairs={{0,4},{4,8},{8,12},{12,16},{16,20},{20,24},{24,28},{1,5},{5,9},{9,... | collective-permute-start | bytes 589832 | tf_op jit(solution)/shard_map/ppermute | solution.py:38
  65.9 17.2 %collective-permute-start.12 = (f32[2,2,96,10,1]{2,1,4,3,0:T(2,128)S(1)}, f32[2,2,96,10,1]{2,1,4,3,0:T(2,128)S(1)}, u32[]{:S(2)}, u32[]{:S(2)}) collective-permute-start(f32[2,2,96,10,1]{2,1,4,3,0:T(2,128)S(1)} %copy.199), channel_id=1, source_target_pairs={{0,1},{1,2},{2,3},{4,5},{5,6},{6,7},{8,9},{9,10},{10,11},{12,13},{... | collective-permute-start | bytes 46088 | tf_op jit(solution)/shard_map/ppermute | solution.py:38
  71.2 6.0 %copy-start.31 = (f32[96,8,128]{2,0,1:T(8,128)S(1)}, f32[96,8,128]{2,0,1:T(8,128)}, u32[]{:S(2)}) copy-start(f32[96,8,128]{2,0,1:T(8,128)} %get-tuple-element.24) | copy-start | bytes 1179652
  71.2 7.0 %copy-start.30 = (f32[96,8,128]{2,0,1:T(8,128)S(1)}, f32[96,8,128]{2,0,1:T(8,128)}, u32[]{:S(2)}) copy-start(f32[96,8,128]{2,0,1:T(8,128)} %get-tuple-element.23) | copy-start | bytes 1179652
  71.2 14.3 %collective-permute-start.11 = (f32[2,2,96,10,1]{2,1,4,3,0:T(2,128)}, f32[2,2,96,10,1]{2,1,4,3,0:T(2,128)}, u32[]{:S(2)}, u32[]{:S(2)}) collective-permute-start(f32[2,2,96,10,1]{2,1,4,3,0:T(2,128)} %copy.196), channel_id=1, source_target_pairs={{1,0},{2,1},{3,2},{5,4},{6,5},{7,6},{9,8},{10,9},{11,10},{13,12},{... | collective-permute-start | bytes 46088 | tf_op jit(solution)/shard_map/ppermute | solution.py:39
  75.0 4.1 %copy-start.29 = (f32[96,8,128]{2,0,1:T(8,128)S(1)}, f32[96,8,128]{2,0,1:T(8,128)}, u32[]{:S(2)}) copy-start(f32[96,8,128]{2,0,1:T(8,128)} %get-tuple-element.22) | copy-start | bytes 1179652
  77.2 3.0 %copy-start.28 = (f32[96,8,128]{2,0,1:T(8,128)S(1)}, f32[96,8,128]{2,0,1:T(8,128)}, u32[]{:S(2)}) copy-start(f32[96,8,128]{2,0,1:T(8,128)} %get-tuple-element.21) | copy-start | bytes 1179652
  77.2 4.0 %copy-start.27 = (f32[96,8,128]{2,0,1:T(8,128)S(1)}, f32[96,8,128]{2,0,1:T(8,128)}, u32[]{:S(2)}) copy-start(f32[96,8,128]{2,0,1:T(8,128)} %get-tuple-element.19) | copy-start | bytes 1179652
  78.1 4.0 %copy-start.26 = (f32[96,8,128]{2,0,1:T(8,128)S(1)}, f32[96,8,128]{2,0,1:T(8,128)}, u32[]{:S(2)}) copy-start(f32[96,8,128]{2,0,1:T(8,128)} %get-tuple-element.20) | copy-start | bytes 1179652
  88.5 6.0 %copy-start.4 = (f32[96,8,128]{2,1,0:T(8,128)S(1)}, f32[96,8,128]{2,1,0:T(8,128)}, u32[]{:S(2)}) copy-start(f32[96,8,128]{2,1,0:T(8,128)} %copy-done.3) | copy-start | bytes 1179652
  88.5 6.0 %copy-start.10 = (f32[96,8,128]{2,1,0:T(8,128)S(1)}, f32[96,8,128]{2,1,0:T(8,128)}, u32[]{:S(2)}) copy-start(f32[96,8,128]{2,1,0:T(8,128)} %copy-done.9) | copy-start | bytes 1179652
  88.5 6.0 %copy-start.16 = (f32[96,8,128]{2,1,0:T(8,128)S(1)}, f32[96,8,128]{2,1,0:T(8,128)}, u32[]{:S(2)}) copy-start(f32[96,8,128]{2,1,0:T(8,128)} %copy-done.15) | copy-start | bytes 1179652
  96.4 16.4 %copy-start.5 = (f32[96,8,128]{2,1,0:T(8,128)S(1)}, f32[96,8,128]{2,1,0:T(8,128)}, u32[]{:S(2)}) copy-start(f32[96,8,128]{2,1,0:T(8,128)} %copy-done.3) | copy-start | bytes 1179652
  96.4 16.4 %copy-start.11 = (f32[96,8,128]{2,1,0:T(8,128)S(1)}, f32[96,8,128]{2,1,0:T(8,128)}, u32[]{:S(2)}) copy-start(f32[96,8,128]{2,1,0:T(8,128)} %copy-done.9) | copy-start | bytes 1179652
  96.4 16.5 %copy-start.17 = (f32[96,8,128]{2,1,0:T(8,128)S(1)}, f32[96,8,128]{2,1,0:T(8,128)}, u32[]{:S(2)}) copy-start(f32[96,8,128]{2,1,0:T(8,128)} %copy-done.15) | copy-start | bytes 1179652
  96.4 16.5 %copy-start.24 = (f32[96,8,128]{2,1,0:T(8,128)S(1)}, f32[96,8,128]{2,1,0:T(8,128)}, u32[]{:S(2)}) copy-start(f32[96,8,128]{2,1,0:T(8,128)} %copy-done.23) | copy-start | bytes 1179652
  99.2 3.6 %collective-permute-start.13 = (f32[1,2,2,2,16]{4,3,2,1,0:T(2,128)S(1)}, f32[1,2,2,2,16]{4,3,2,1,0:T(2,128)S(1)}, u32[]{:S(2)}, u32[]{:S(2)}) collective-permute-start(f32[1,2,2,2,16]{4,3,2,1,0:T(2,128)S(1)} %bitcast.155), channel_id=1, source_target_pairs={{0,1},{1,0},{2,3},{3,2},{4,5},{5,4},{6,7},{7,6},{8,9},{9,8},{10,11... | collective-permute-start | bytes 1544 | tf_op jit(solution)/shard_map/ppermute | solution.py:20
  102.8 4.6 %collective-permute-start.14 = (f32[2,2,2,2,16]{4,3,2,1,0:T(2,128)S(1)}, f32[2,2,2,2,16]{4,3,2,1,0:T(2,128)S(1)}, u32[]{:S(2)}, u32[]{:S(2)}) collective-permute-start(f32[2,2,2,2,16]{4,3,2,1,0:T(2,128)S(1)} %maximum_select_fusion.13), channel_id=1, source_target_pairs={{0,2},{1,3},{2,0},{3,1},{4,6},{5,7},{6,4},{7,5},{8,10},{9,11},{10,... | collective-permute-start | bytes 3080 | tf_op jit(solution)/shard_map/ppermute | solution.py:20
  107.4 1.2 collective-permute-start.15
  108.7 4.0 %collective-permute-start.16 = (f32[8,2,2,2,16]{4,3,2,1,0:T(2,128)S(1)}, f32[8,2,2,2,16]{4,3,2,1,0:T(2,128)S(1)}, u32[]{:S(2)}, u32[]{:S(2)}) collective-permute-start(f32[8,2,2,2,16]{4,3,2,1,0:T(2,128)S(1)} %maximum_select_fusion.7), channel_id=1, source_target_pairs={{0,8},{1,9},{2,10},{3,11},{4,12},{5,13},{6,14},{7,15},{8,0},{9,1},... | collective-permute-start | bytes 12296 | tf_op jit(solution)/shard_map/ppermute | solution.py:20
  112.7 4.3 %collective-permute-start.17 = (f32[16,2,2,2,16]{4,3,2,1,0:T(2,128)S(1)}, f32[16,2,2,2,16]{4,3,2,1,0:T(2,128)S(1)}, u32[]{:S(2)}, u32[]{:S(2)}) collective-permute-start(f32[16,2,2,2,16]{4,3,2,1,0:T(2,128)S(1)} %maximum_select_fusion.4), channel_id=1, source_target_pairs={{0,16},{1,17},{2,18},{3,19},{4,20},{5,21},{6,22},{7,23},{8,24},{9,... | collective-permute-start | bytes 24584 | tf_op jit(solution)/shard_map/ppermute | solution.py:20
  125.3 7.2 %collective-permute-start.18 = (f32[2,2,96,1,128]{4,3,2,1,0:T(1,128)S(1)}, f32[2,2,96,1,128]{4,3,2,1,0:T(1,128)S(1)}, u32[]{:S(2)}, u32[]{:S(2)}) collective-permute-start(f32[2,2,96,1,128]{4,3,2,1,0:T(1,128)S(1)} %get-tuple-element.62), channel_id=1, source_target_pairs={{4,0},{8,4},{12,8},{16,12},{20,16},{24,20},{28,24},{5,1},{9,5},{13... | collective-permute-start | bytes 589832 | tf_op jit(solution)/shard_map/ppermute | solution.py:39
  127.2 7.9 %collective-permute-start.19 = (f32[2,2,96,1,128]{4,3,2,1,0:T(1,128)S(1)}, f32[2,2,96,1,128]{4,3,2,1,0:T(1,128)S(1)}, u32[]{:S(2)}, u32[]{:S(2)}) collective-permute-start(f32[2,2,96,1,128]{4,3,2,1,0:T(1,128)S(1)} %get-tuple-element.61), channel_id=1, source_target_pairs={{0,4},{4,8},{8,12},{12,16},{16,20},{20,24},{24,28},{1,5},{5,9},{9,... | collective-permute-start | bytes 589832 | tf_op jit(solution)/shard_map/ppermute | solution.py:38
  142.3 11.1 %collective-permute-start.21 = (f32[2,2,96,10,1]{2,1,4,3,0:T(2,128)S(1)}, f32[2,2,96,10,1]{2,1,4,3,0:T(2,128)S(1)}, u32[]{:S(2)}, u32[]{:S(2)}) collective-permute-start(f32[2,2,96,10,1]{2,1,4,3,0:T(2,128)S(1)} %copy.208), channel_id=1, source_target_pairs={{0,1},{1,2},{2,3},{4,5},{5,6},{6,7},{8,9},{9,10},{10,11},{12,13},{... | collective-permute-start | bytes 46088 | tf_op jit(solution)/shard_map/ppermute | solution.py:38
  147.6 8.1 %collective-permute-start.20 = (f32[2,2,96,10,1]{2,1,4,3,0:T(2,128)}, f32[2,2,96,10,1]{2,1,4,3,0:T(2,128)}, u32[]{:S(2)}, u32[]{:S(2)}) collective-permute-start(f32[2,2,96,10,1]{2,1,4,3,0:T(2,128)} %copy.206), channel_id=1, source_target_pairs={{1,0},{2,1},{3,2},{5,4},{6,5},{7,6},{9,8},{10,9},{11,10},{13,12},{... | collective-permute-start | bytes 46088 | tf_op jit(solution)/shard_map/ppermute | solution.py:39
  158.8 6.0 %copy-start.6 = (f32[96,8,128]{2,1,0:T(8,128)S(1)}, f32[96,8,128]{2,1,0:T(8,128)}, u32[]{:S(2)}) copy-start(f32[96,8,128]{2,1,0:T(8,128)} %copy-done.3) | copy-start | bytes 1179652
  158.8 6.0 %copy-start.12 = (f32[96,8,128]{2,1,0:T(8,128)S(1)}, f32[96,8,128]{2,1,0:T(8,128)}, u32[]{:S(2)}) copy-start(f32[96,8,128]{2,1,0:T(8,128)} %copy-done.9) | copy-start | bytes 1179652
  158.8 6.0 %copy-start.18 = (f32[96,8,128]{2,1,0:T(8,128)S(1)}, f32[96,8,128]{2,1,0:T(8,128)}, u32[]{:S(2)}) copy-start(f32[96,8,128]{2,1,0:T(8,128)} %copy-done.15) | copy-start | bytes 1179652
  158.8 6.0 %copy-start.37 = (f32[2]{0:T(128)S(1)}, f32[2]{0:T(128)}, u32[]{:S(2)}) copy-start(f32[2]{0:T(128)} %param.12) | copy-start | bytes 28
  166.7 16.4 %copy-start.7 = (f32[96,8,128]{2,1,0:T(8,128)S(1)}, f32[96,8,128]{2,1,0:T(8,128)}, u32[]{:S(2)}) copy-start(f32[96,8,128]{2,1,0:T(8,128)} %copy-done.3) | copy-start | bytes 1179652
  166.7 16.4 %copy-start.13 = (f32[96,8,128]{2,1,0:T(8,128)S(1)}, f32[96,8,128]{2,1,0:T(8,128)}, u32[]{:S(2)}) copy-start(f32[96,8,128]{2,1,0:T(8,128)} %copy-done.9) | copy-start | bytes 1179652
  166.7 16.5 %copy-start.19 = (f32[96,8,128]{2,1,0:T(8,128)S(1)}, f32[96,8,128]{2,1,0:T(8,128)}, u32[]{:S(2)}) copy-start(f32[96,8,128]{2,1,0:T(8,128)} %copy-done.15) | copy-start | bytes 1179652
  166.7 16.5 %copy-start.25 = (f32[96,8,128]{2,1,0:T(8,128)S(1)}, f32[96,8,128]{2,1,0:T(8,128)}, u32[]{:S(2)}) copy-start(f32[96,8,128]{2,1,0:T(8,128)} %copy-done.23) | copy-start | bytes 1179652
  169.5 3.6 %collective-permute-start.22 = (f32[1,2,2,2,16]{4,3,2,1,0:T(2,128)S(1)}, f32[1,2,2,2,16]{4,3,2,1,0:T(2,128)S(1)}, u32[]{:S(2)}, u32[]{:S(2)}) collective-permute-start(f32[1,2,2,2,16]{4,3,2,1,0:T(2,128)S(1)} %bitcast.153), channel_id=1, source_target_pairs={{0,1},{1,0},{2,3},{3,2},{4,5},{5,4},{6,7},{7,6},{8,9},{9,8},{10,11... | collective-permute-start | bytes 1544 | tf_op jit(solution)/shard_map/ppermute | solution.py:20
  173.1 4.6 %collective-permute-start.23 = (f32[2,2,2,2,16]{4,3,2,1,0:T(2,128)S(1)}, f32[2,2,2,2,16]{4,3,2,1,0:T(2,128)S(1)}, u32[]{:S(2)}, u32[]{:S(2)}) collective-permute-start(f32[2,2,2,2,16]{4,3,2,1,0:T(2,128)S(1)} %maximum_select_fusion.14), channel_id=1, source_target_pairs={{0,2},{1,3},{2,0},{3,1},{4,6},{5,7},{6,4},{7,5},{8,10},{9,11},{10,... | collective-permute-start | bytes 3080 | tf_op jit(solution)/shard_map/ppermute | solution.py:20
  177.7 1.2 collective-permute-start.24
  179.0 4.0 %collective-permute-start.25 = (f32[8,2,2,2,16]{4,3,2,1,0:T(2,128)S(1)}, f32[8,2,2,2,16]{4,3,2,1,0:T(2,128)S(1)}, u32[]{:S(2)}, u32[]{:S(2)}) collective-permute-start(f32[8,2,2,2,16]{4,3,2,1,0:T(2,128)S(1)} %maximum_select_fusion.8), channel_id=1, source_target_pairs={{0,8},{1,9},{2,10},{3,11},{4,12},{5,13},{6,14},{7,15},{8,0},{9,1},... | collective-permute-start | bytes 12296 | tf_op jit(solution)/shard_map/ppermute | solution.py:20
  183.0 4.3 %collective-permute-start.26 = (f32[16,2,2,2,16]{4,3,2,1,0:T(2,128)S(1)}, f32[16,2,2,2,16]{4,3,2,1,0:T(2,128)S(1)}, u32[]{:S(2)}, u32[]{:S(2)}) collective-permute-start(f32[16,2,2,2,16]{4,3,2,1,0:T(2,128)S(1)} %maximum_select_fusion.5), channel_id=1, source_target_pairs={{0,16},{1,17},{2,18},{3,19},{4,20},{5,21},{6,22},{7,23},{8,24},{9,... | collective-permute-start | bytes 24584 | tf_op jit(solution)/shard_map/ppermute | solution.py:20
  194.6 42.4 %copy-start.1 = (f32[2,2,96,8,128]{4,3,2,1,0:T(8,128)}, f32[2,2,96,8,128]{4,3,2,1,0:T(8,128)S(1)}, u32[]{:S(2)}) copy-start(f32[2,2,96,8,128]{4,3,2,1,0:T(8,128)S(1)} %fusion.28) | copy-start | bytes 4718596
  196.7 7.3 %collective-permute-start.27 = (f32[2,2,96,1,128]{4,3,2,1,0:T(1,128)S(1)}, f32[2,2,96,1,128]{4,3,2,1,0:T(1,128)S(1)}, u32[]{:S(2)}, u32[]{:S(2)}) collective-permute-start(f32[2,2,96,1,128]{4,3,2,1,0:T(1,128)S(1)} %get-tuple-element.58), channel_id=1, source_target_pairs={{4,0},{8,4},{12,8},{16,12},{20,16},{24,20},{28,24},{5,1},{9,5},{13... | collective-permute-start | bytes 589832 | tf_op jit(solution)/shard_map/ppermute | solution.py:39
  198.6 7.9 %collective-permute-start.28 = (f32[2,2,96,1,128]{4,3,2,1,0:T(1,128)S(1)}, f32[2,2,96,1,128]{4,3,2,1,0:T(1,128)S(1)}, u32[]{:S(2)}, u32[]{:S(2)}) collective-permute-start(f32[2,2,96,1,128]{4,3,2,1,0:T(1,128)S(1)} %get-tuple-element.57), channel_id=1, source_target_pairs={{0,4},{4,8},{8,12},{12,16},{16,20},{20,24},{24,28},{1,5},{5,9},{9,... | collective-permute-start | bytes 589832 | tf_op jit(solution)/shard_map/ppermute | solution.py:38
  214.0 11.3 %collective-permute-start.30 = (f32[2,2,96,10,1]{2,3,4,1,0:T(8,128)S(1)}, f32[2,2,96,10,1]{2,3,4,1,0:T(8,128)S(1)}, u32[]{:S(2)}, u32[]{:S(2)}) collective-permute-start(f32[2,2,96,10,1]{2,3,4,1,0:T(8,128)S(1)} %copy.215), channel_id=1, source_target_pairs={{0,1},{1,2},{2,3},{4,5},{5,6},{6,7},{8,9},{9,10},{10,11},{12,13},{... | collective-permute-start | bytes 46088 | tf_op jit(solution)/shard_map/ppermute | solution.py:38
  219.6 8.2 %collective-permute-start.29 = (f32[2,2,96,10,1]{2,3,4,1,0:T(8,128)}, f32[2,2,96,10,1]{2,3,4,1,0:T(8,128)}, u32[]{:S(2)}, u32[]{:S(2)}) collective-permute-start(f32[2,2,96,10,1]{2,3,4,1,0:T(8,128)} %copy.213), channel_id=1, source_target_pairs={{1,0},{2,1},{3,2},{5,4},{6,5},{7,6},{9,8},{10,9},{11,10},{13,12},{... | collective-permute-start | bytes 46088 | tf_op jit(solution)/shard_map/ppermute | solution.py:39
  230.8 6.2 %copy-start.8 = (f32[96,8,128]{2,1,0:T(8,128)S(1)}, f32[96,8,128]{2,1,0:T(8,128)}, u32[]{:S(2)}) copy-start(f32[96,8,128]{2,1,0:T(8,128)} %copy-done.3) | copy-start | bytes 1179652
  230.8 6.2 %copy-start.14 = (f32[96,8,128]{2,1,0:T(8,128)S(1)}, f32[96,8,128]{2,1,0:T(8,128)}, u32[]{:S(2)}) copy-start(f32[96,8,128]{2,1,0:T(8,128)} %copy-done.9) | copy-start | bytes 1179652
  230.8 6.2 %copy-start.20 = (f32[96,8,128]{2,1,0:T(8,128)S(1)}, f32[96,8,128]{2,1,0:T(8,128)}, u32[]{:S(2)}) copy-start(f32[96,8,128]{2,1,0:T(8,128)} %copy-done.15) | copy-start | bytes 1179652
  (12 other events, 13.2 us)
